TPU v7x, 256 devices: a whole 4x4x8 slice. The times are simulated.
256 devices in a mesh: ctx: 32 (over z, y_lo, core), head: 8 (over y_hi, x).
Axes of the slice: x: 4, y: 4 (y_hi: 2, y_lo: 2; y = y_hi * 2 + y_lo), z: 8, core: 2. Of those that a mesh axis runs over, the one named last changes fastest.
Arguments:
- queries: bfloat16 [6144, 3072], P('ctx', 'head'), may hold values from -6 to 6
- keys: bfloat16 [6144, 3072], P('ctx', 'head'), may hold values from -6 to 6
- values: bfloat16 [6144, 3072], P('ctx', 'head'), may hold values from -6 to 6
- query_tan: bfloat16 [6144, 3072], P('ctx', 'head'), may hold values from -6 to 6
- key_tan: bfloat16 [6144, 3072], P('ctx', 'head'), may hold values from -6 to 6
- value_tan: bfloat16 [6144, 3072], P('ctx', 'head'), may hold values from -6 to 6
- out_weight: bfloat16 [3072, 5120], P('head'), may hold values from -0.109375 to 0.109375
- gate: float32 [5120], P('head'), may hold values from 8 to 64
- gate_tan: float32 [5120], P('head'), may hold values from -96 to 96
Outputs:
- update: bfloat16 [6144, 5120], P('ctx', 'head')
- update_tan: bfloat16 [6144, 5120], P('ctx', 'head')
All inputs are finite; a program needn't handle non-finite values.
Results may differ from a plain program's by a relative error of at most 0.018.
Values may be sent and summed in bfloat16 or wider, within the bound.
A program may use at most 128 MiB of HBM per device.

v0:
```python
import math

import jax
import jax.numpy as jnp
from jax import lax
from jax.sharding import PartitionSpec as P

DH = 128


def pick_block(length):
    for candidate in range(min(length, 1024), 0, -1):
        if length % candidate == 0 and candidate % 128 == 0:
            return candidate
    for candidate in range(min(length, 1024), 0, -1):
        if length % candidate == 0:
            return candidate
    return length


def local(queries, keys, values, query_tan, key_tan, value_tan, out_weight, gate, gate_tan):
    row_count = queries.shape[0]
    head_count = queries.shape[1] // DH
    factor = 1.0 / math.sqrt(DH)
    query_heads = queries.reshape(row_count, head_count, DH).transpose(1, 0, 2)
    tangent_heads = query_tan.reshape(row_count, head_count, DH).transpose(1, 0, 2)

    def blocks_of(pieces):
        length = pieces[0].shape[0]
        span = pick_block(length)
        return tuple((piece.reshape(length // span, span, head_count, DH) for piece in pieces))

    def plain_scores(key_block):
        return (
            jnp.einsum("hqd,khd->hqk", query_heads, key_block, preferred_element_type=jnp.float32)
            * factor
        )

    def tangent_scores(key_block, key_tan_block):
        first_term = jnp.einsum(
            "hqd,khd->hqk", tangent_heads, key_block, preferred_element_type=jnp.float32
        )
        second_term = jnp.einsum(
            "hqd,khd->hqk", query_heads, key_tan_block, preferred_element_type=jnp.float32
        )
        return (first_term + second_term) * factor

    def value_sums(weights, mixed_weights, value_block, value_tan_block):
        plain_sum = jnp.einsum(
            "hqk,khd->hqd", weights, value_block, preferred_element_type=jnp.float32
        )
        tan_sum = jnp.einsum(
            "hqk,khd->hqd", weights, value_tan_block, preferred_element_type=jnp.float32
        )
        tan_sum = tan_sum + jnp.einsum(
            "hqk,khd->hqd", mixed_weights, value_block, preferred_element_type=jnp.float32
        )
        return (plain_sum, tan_sum)

    lowest = jnp.full((head_count, row_count), -1e30, jnp.float32)
    empty_rows = jnp.zeros((head_count, row_count), jnp.float32)
    empty_heads = jnp.zeros((head_count, row_count, DH), jnp.float32)

    def max_step(running, block_parts):
        old_max, normalizer = running
        scores = plain_scores(block_parts[0])
        new_max = jnp.maximum(old_max, jnp.max(scores, axis=-1))
        normalizer = jnp.exp(old_max - new_max) * normalizer + jnp.sum(
            jnp.exp(scores - new_max[..., None]), axis=-1
        )
        return ((new_max, normalizer), None)

    running = (lowest, empty_rows)
    running, unused = lax.scan(
        max_step, running, blocks_of((lax.all_gather(keys, "ctx", axis=0, tiled=True),))
    )
    row_max, normalizer = running

    def fixed_step(running, block_parts):
        slope_sum, weighted, weighted_tan = running
        key_block, value_block, key_tan_block, value_tan_block = block_parts
        scores = plain_scores(key_block)
        score_tan = tangent_scores(key_block, key_tan_block)
        exponent = jnp.exp(scores - row_max[..., None])
        mixed_terms = exponent * score_tan
        plain_sum, tan_sum = value_sums(
            exponent.astype(jnp.bfloat16),
            mixed_terms.astype(jnp.bfloat16),
            value_block,
            value_tan_block,
        )
        return (
            (
                slope_sum + jnp.sum(mixed_terms, axis=-1),
                weighted + plain_sum,
                weighted_tan + tan_sum,
            ),
            None,
        )

    running = (empty_rows, empty_heads, empty_heads)
    running, unused = lax.scan(
        fixed_step,
        running,
        blocks_of(
            (
                lax.all_gather(keys, "ctx", axis=0, tiled=True),
                lax.all_gather(values, "ctx", axis=0, tiled=True),
                lax.all_gather(key_tan, "ctx", axis=0, tiled=True),
                lax.all_gather(value_tan, "ctx", axis=0, tiled=True),
            )
        ),
    )
    slope_sum, weighted, weighted_tan = running
    attention_full = weighted / normalizer[..., None]
    slope_mean = slope_sum / normalizer
    attention_tan_full = (
        weighted_tan / normalizer[..., None] - attention_full * slope_mean[..., None]
    )
    attention = (
        attention_full.astype(jnp.bfloat16).transpose(1, 0, 2).reshape(row_count, head_count * DH)
    )
    attention_tan = (
        attention_tan_full.astype(jnp.bfloat16)
        .transpose(1, 0, 2)
        .reshape(row_count, head_count * DH)
    )
    stacked = jnp.concatenate((attention, attention_tan), axis=0)
    summed = lax.psum_scatter(
        lax.dot_general(
            out_weight, stacked, (((0,), (1,)), ((), ())), preferred_element_type=jnp.float32
        ).astype(jnp.bfloat16),
        "head",
        scatter_dimension=0,
        tiled=True,
    ).astype(jnp.float32)
    projected = summed[:, :row_count].T
    projected_tan = summed[:, row_count:].T
    update = (gate[None, :] * projected).astype(jnp.bfloat16)
    update_tan = (gate_tan[None, :] * projected + gate[None, :] * projected_tan).astype(
        jnp.bfloat16
    )
    return (update, update_tan)


def solution(mesh):
    in_specs = (
        P("ctx", "head"),
        P("ctx", "head"),
        P("ctx", "head"),
        P("ctx", "head"),
        P("ctx", "head"),
        P("ctx", "head"),
        P("head", None),
        P("head"),
        P("head"),
    )
    out_specs = (P("ctx", "head"), P("ctx", "head"))
    return jax.shard_map(local, mesh=mesh, in_specs=in_specs, out_specs=out_specs, check_vma=False)
```

profile of v0, /device:TPU:1, one launch (start us, length us, event | category | flops | bytes accessed | tf_op | source)
XLA Modules:
  0.0 481.0 jit_solution(2285477850434179948)
XLA Ops:
  12.0 70.1 %all-gather.5.cloned.1.call-done = bf16[6144,384]{1,0:T(8,128)(2,1)} async-done(((bf16[192,384]{1,0:T(8,128)(2,1)}), bf16[6144,384]{1,0:T(8,128)(2,1)}) %all-gather.5.cloned.1.call-update) | async-done | bytes 4718608 | tf_op jit(solution)/shard_map/all_gather | solution.py:107
  82.1 12.9 %reshape.48 = bf16[6,1024,3,128]{3,2,1,0:T(4,128)(2,1)} reshape(bf16[6144,384]{1,0:T(8,128)(2,1)} %all-gather.5.cloned.1.call-done) | data formatting | bytes 9437184 | tf_op jit(solution)/shard_map/reshape | solution.py:31
  95.0 6.1 %copy.31 = bf16[6,1024,3,128]{3,1,2,0:T(8,128)(2,1)} copy(bf16[6,1024,3,128]{3,2,1,0:T(4,128)(2,1)} %reshape.48) | data formatting | bytes 9437184
  101.1 50.3 %all-gather.7.cloned.1.call-done = bf16[6144,384]{1,0:T(8,128)(2,1)} async-done(((bf16[192,384]{1,0:T(8,128)(2,1)}), bf16[6144,384]{1,0:T(8,128)(2,1)}) %all-gather.7.cloned.1.call-update) | async-done | bytes 4718608 | tf_op jit(solution)/shard_map/all_gather | solution.py:109
  151.4 12.9 %reshape.43 = bf16[6,1024,3,128]{3,2,1,0:T(4,128)(2,1)} reshape(bf16[6144,384]{1,0:T(8,128)(2,1)} %all-gather.7.cloned.1.call-done) | data formatting | bytes 9437184 | tf_op jit(solution)/shard_map/reshape | solution.py:31
  164.4 6.0 %copy.34 = bf16[6,1024,3,128]{3,1,2,0:T(8,128)(2,1)} copy(bf16[6,1024,3,128]{3,2,1,0:T(4,128)(2,1)} %reshape.43) | data formatting | bytes 9437184
  170.4 50.4 %all-gather.9.cloned.1.call-done = bf16[6144,384]{1,0:T(8,128)(2,1)} async-done(((bf16[192,384]{1,0:T(8,128)(2,1)}), bf16[6144,384]{1,0:T(8,128)(2,1)}) %all-gather.9.cloned.1.call-update) | async-done | bytes 4718608 | tf_op jit(solution)/shard_map/all_gather | solution.py:108
  220.8 12.9 %reshape.44 = bf16[6,1024,3,128]{3,2,1,0:T(4,128)(2,1)} reshape(bf16[6144,384]{1,0:T(8,128)(2,1)} %all-gather.9.cloned.1.call-done) | data formatting | bytes 9437184 | tf_op jit(solution)/shard_map/reshape | solution.py:31
  233.7 6.0 %copy.35 = bf16[6,1024,3,128]{3,1,2,0:T(8,128)(2,1)} copy(bf16[6,1024,3,128]{3,2,1,0:T(4,128)(2,1)} %reshape.44) | data formatting | bytes 9437184
  239.8 13.9 %while.28 = (s32[]{:T(128)}, f32[3,192]{1,0:T(4,128)S(1)}, f32[3,192]{1,0:T(4,128)S(1)}, bf16[6,1024,3,128]{3,1,2,0:T(8,128)(2,1)}, bf16[3,192,128]{2,1,0:T(8,128)(2,1)S(1)}, /*index=5*/s32[]{:T(128)}, s32[]{:T(128)}) while((s32[]{:T(128)}, f32[3,192]{1,0:T(4,128)S(1)}, f32[3,192]{1,0:T(4,128)S(1)}, ...), condition=%wide.region_3.4_spmd.clone, body=%wide.region_0.3_spmd.clone.sunk | while | flops 153946944 | bytes 5683032 | solution.py:74
  253.7 36.3 %all-gather.11.cloned.1.call-done = bf16[6144,384]{1,0:T(8,128)(2,1)} async-done(((bf16[192,384]{1,0:T(8,128)(2,1)}), bf16[6144,384]{1,0:T(8,128)(2,1)}) %all-gather.11.cloned.1.call-update) | async-done | bytes 4718608 | tf_op jit(solution)/shard_map/all_gather | solution.py:110
  290.0 12.9 %reshape.45 = bf16[6,1024,3,128]{3,2,1,0:T(4,128)(2,1)} reshape(bf16[6144,384]{1,0:T(8,128)(2,1)} %all-gather.11.cloned.1.call-done) | data formatting | bytes 9437184 | tf_op jit(solution)/shard_map/reshape | solution.py:31
  302.9 6.1 %copy.36 = bf16[6,1024,3,128]{3,1,2,0:T(8,128)(2,1)} copy(bf16[6,1024,3,128]{3,2,1,0:T(4,128)(2,1)} %reshape.45) | data formatting | bytes 9437184
  309.1 63.5 %while.29 = (s32[]{:T(128)}, f32[3,192]{1,0:T(4,128)S(1)}, f32[3,192,128]{2,1,0:T(8,128)S(1)}, f32[3,192,128]{2,1,0:T(8,128)S(1)}, bf16[6,1024,3,128]{3,1,2,0:T(...) while((s32[]{:T(128)}, f32[3,192]{1,0:T(4,128)S(1)}, ...), condition=%wide.region_6.7_spmd.clone, body=%wide.region_4.6_spmd.clone.sunk | while | flops 914006592 | bytes 23464840 | solution.py:102
  312.3 2.1 bitcast_reduce_fusion.5
  316.0 1.8 fusion.86
  322.9 2.1 bitcast_reduce_fusion.5
  333.5 2.1 bitcast_reduce_fusion.5
  344.1 2.1 bitcast_reduce_fusion.5
  354.7 2.1 bitcast_reduce_fusion.5
  365.3 2.1 bitcast_reduce_fusion.5
  372.9 6.2 %fusion.34 = bf16[5120,384]{0,1:T(8,128)(2,1)} fusion(bf16[384,5120]{1,0:T(8,128)(2,1)} %param.19, bf16[192,384]{1,0:T(8,128)(2,1)S(1)} %get-tuple-element.220, bf16[192,384]{1,0:T(8,128)(2,1)S(1)} %get-tuple-element.221), kind=kOutput, calls=%fused_computation.44 | convolution fusion | flops 1512505344 | bytes 8159232 | tf_op jit(solution)/shard_map/dot_general | solution.py:130
  379.1 6.3 %copy.45 = bf16[5120,384]{1,0:T(8,128)(2,1)} copy(bf16[5120,384]{0,1:T(8,128)(2,1)} %fusion.34) | data formatting | bytes 7864320
  385.4 86.8 %reduce-scatter.4.cloned.1.call-done = bf16[640,384]{1,0:T(8,128)(2,1)} async-done(((bf16[5120,384]{1,0:T(8,128)(2,1)}), bf16[640,384]{1,0:T(8,128)(2,1)}) %reduce-scatter.4.cloned.1.call-update) | async-done | bytes 491536
  (94 shorter events, 69.7 us)
Async XLA Ops:
  7.2 74.9 %all-gather.5.cloned.1.call-start = ((), (), s32[]{:S(2)}) async-start(), calls=%async_computation.1 | async-start | bytes 4866048 | tf_op jit(solution)/shard_map/all_gather | solution.py:107
  7.9 143.6 %all-gather.7.cloned.1.call-start = ((), (), s32[]{:S(2)}) async-start(), calls=%async_computation.2 | async-start | bytes 4866048 | tf_op jit(solution)/shard_map/all_gather | solution.py:109
  8.6 212.2 %all-gather.9.cloned.1.call-start = ((), (), s32[]{:S(2)}) async-start(), calls=%async_computation.3 | async-start | bytes 4866048 | tf_op jit(solution)/shard_map/all_gather | solution.py:108
  9.4 280.6 %all-gather.11.cloned.1.call-start = ((), (), s32[]{:S(2)}) async-start(), calls=%async_computation.4 | async-start | bytes 4866048 | tf_op jit(solution)/shard_map/all_gather | solution.py:110
  10.0 462.3 %reduce-scatter.4.cloned.1.call-start = ((), (), s32[]{:S(2)}) async-start(), calls=%async_computation.5 | async-start | bytes 4423680
  385.4 88.2 %copy-start = (f32[640]{0:T(1024)S(1)}, f32[640]{0:T(1024)}, u32[]{:S(2)}) copy-start(f32[640]{0:T(1024)} %param.21) | copy-start | bytes 7684
  385.4 88.2 %copy-start.1 = (f32[640]{0:T(1024)S(1)}, f32[640]{0:T(1024)}, u32[]{:S(2)}) copy-start(f32[640]{0:T(1024)} %param.20) | copy-start | bytes 7684
Sparse Core Ops, SparseCore 0:
  9.9 72.2 all-gather.4
  84.0 67.4 all-gather.6
  153.3 67.4 all-gather.8
  222.5 67.4 all-gather.10
  385.6 86.6 reduce-scatter.3
where the time goes:
time: 485 us; the launch traced here: 481 us
  waiting for transfers between devices  296 us (61%)
  local copies, waits for them, and re-layouts  85.6 us (18%)
  matrix products  79.6 us (16%)
  between operations  13.9 us (3%)
    unnamed x6, waiting for transfers between devices  89.4 us
    all_gather x1, waiting for transfers between devices, local(): lax.all_gather(keys, 'ctx', axis=0, tiled=True)  70.1 us
    reshape x4, local copies, waits for them, and re-layouts, blocks_of(): piece.reshape(length // span, span, head_count, DH)  51.8 us
    all_gather x1, waiting for transfers between devices, local(): lax.all_gather(values, 'ctx', axis=0, tiled=True)  50.4 us
    all_gather x1, waiting for transfers between devices, local(): lax.all_gather(key_tan, 'ctx', axis=0, tiled=True)  50.3 us
    all_gather x1, waiting for transfers between devices, local(): lax.all_gather(value_tan, 'ctx', axis=0, tiled=True)  36.3 us
    unnamed x12, local copies, waits for them, and re-layouts  31.9 us
    dot_general x12, matrix products, plain_scores(): jnp.einsum('hqd,khd->hqk', query_heads, key_block, preferred_element_type...  19.8 us
  transfers between devices with their start and end apart: 5, of which 5 were waited for; matrix products, arithmetic and copies ran while one was open for 15% of the time, Pallas kernels for 0%

commit v1 on v0

v1 whole, which is shorter than its diff:
```python
import functools
import math

import jax
import jax.numpy as jnp
from jax import lax
from jax.experimental import pallas as pl
from jax.experimental.pallas import tpu as pltpu
from jax.sharding import PartitionSpec as P

DH = 128
HEADS = 3
RING = 8
WIDE = 4
FACTOR = 1.0 / math.sqrt(DH)
BASE2 = FACTOR * math.log2(math.e)
MESH = pl.DeviceIdType.MESH
F32 = jnp.float32
BF16 = jnp.bfloat16
NT = (((1,), (1,)), ((), ()))
NN = (((1,), (0,)), ((), ()))


def kernel(
    rows,
    width,
    queries,
    keys,
    values,
    query_tan,
    key_tan,
    value_tan,
    out_weight,
    gate,
    gate_tan,
    update,
    update_tan,
    qq,
    kv,
    wbuf,
    abuf,
    top,
    norm,
    slope,
    total,
    own,
    own_lse,
    own_slope,
    part,
    part_got,
    stat,
    stat_got,
    acc,
    load_sem,
    q_sem,
    ring_send,
    ring_recv,
    sib_send,
    sib_recv,
    first_sem,
    w_send,
    w_recv,
    w_sib_send,
    w_sib_recv,
    part_sem,
    att_send,
    att_recv,
):
    half = rows // 2
    i = lax.axis_index("ctx")
    g = lax.axis_index("head")
    z, y, c = i // 4, (i // 2) % 2, i % 2
    yh, x = g // WIDE, g % WIDE
    ahead = (((z + 1) % RING) * 4 + y * 2 + c, g)
    behind = (((z + RING - 1) % RING) * 4 + y * 2 + c, g)
    sibling = (z * 4 + y * 2 + 1 - c, g)
    partner = (z * 4 + (1 - y) * 2 + c, g)

    def peer(r):
        return (i, ((yh + r // WIDE) % 2) * WIDE + (x + r % WIDE) % WIDE)

    def back(r):
        return (r // WIDE) * WIDE + (WIDE - r % WIDE) % WIDE

    loads = []

    def load(src, dst):
        copy = pltpu.make_async_copy(src, dst, load_sem.at[len(loads)])
        copy.start()
        loads.append(copy)

    def cols(h):
        return pl.ds(h * DH, DH)

    for h in range(HEADS):
        for pair, low, high in ((0, keys, key_tan), (1, values, value_tan)):
            load(low.at[:, cols(h)], kv.at[0, h, pair, c, :, pl.ds(0, DH)])
            load(high.at[:, cols(h)], kv.at[0, h, pair, c, :, pl.ds(DH, DH)])
    for h in range(HEADS):
        load(query_tan.at[:, cols(h)], qq.at[h, 0, :, pl.ds(0, DH)])
        load(queries.at[:, cols(h)], qq.at[h, 0, :, pl.ds(DH, DH)])
    load(out_weight.at[:, :, pl.ds(pl.multiple_of(g * width, 128), width)], wbuf.at[:, 0])

    barrier = pltpu.get_barrier_semaphore()
    others = [ahead, behind, sibling, partner] + [peer(r) for r in range(1, 2 * WIDE)]
    for other in others:
        pl.semaphore_signal(barrier, inc=1, device_id=other, device_id_type=MESH)
    pl.semaphore_wait(barrier, len(others))

    def remote(src, dst, send, recv, device):
        return pltpu.make_async_remote_copy(
            src_ref=src,
            dst_ref=dst,
            send_sem=send,
            recv_sem=recv,
            device_id=device,
            device_id_type=MESH,
        )

    def slot_of(d, s):
        return 0 if s == 0 else (7 if s == 4 else 2 * s - 1 + d)

    def piece(d, h, s, part_index):
        return kv.at[slot_of(d, s), h, :, c, pl.ds(part_index * half, half)]

    def ring(d, h, s, p):
        tag = 2 * (s - 1) + (p if s < 4 else 0)
        return remote(
            piece(d, h, s - 1, p),
            piece(d, h, s, p),
            ring_send.at[d, h, tag],
            ring_recv.at[d, h, tag],
            ahead if d == 0 else behind,
        )

    def twin(d, h, s, p):
        tag = 2 * (s - 1) + (p if s < 4 else 0)
        ref = piece(d, h, s, p)
        return remote(ref, ref, sib_send.at[d, h, tag], sib_recv.at[d, h, tag], sibling)

    def twin_got(d, h, s, p):
        tag = 2 * (s - 1) + (p if s < 4 else 0)
        ref = kv.at[slot_of(d, s), h, :, 1 - c, pl.ds(p * half, half)]
        return remote(ref, ref, sib_send.at[d, h, tag], sib_recv.at[d, h, tag], sibling)

    def first(h, core):
        ref = kv.at[0, h, :, core]
        return remote(ref, ref, first_sem.at[0, h], first_sem.at[1, h], sibling)

    def query_copy():
        return remote(qq.at[:, 0], qq.at[:, 1], q_sem.at[0], q_sem.at[1], partner)

    share = DH // 2

    def weight(r):
        column = peer(r)[1] * width
        return remote(
            out_weight.at[:, pl.ds(c * share, share), pl.ds(pl.multiple_of(column, 128), width)],
            wbuf.at[:, back(r), pl.ds(c * share, share)],
            w_send.at[r],
            w_recv.at[back(r)],
            peer(r),
        )

    def weight_got(r):
        ref = wbuf.at[:, r, pl.ds(c * share, share)]
        return remote(ref, ref, w_send.at[r], w_recv.at[r], peer(r))

    def weight_twin(r, core):
        ref = wbuf.at[:, r, pl.ds(core * share, share)]
        return remote(ref, ref, w_sib_send.at[r], w_sib_recv.at[r], sibling)

    def part_copies(h):
        return (
            remote(part.at[h], part_got.at[h], part_sem.at[0, h, 0], part_sem.at[1, h, 0], partner),
            remote(stat.at[h], stat_got.at[h], part_sem.at[0, h, 1], part_sem.at[1, h, 1], partner),
        )

    def attention_copy(h, r):
        return remote(
            abuf.at[h, :, :, pl.ds(0, DH)],
            abuf.at[h, :, :, pl.ds(back(r) * DH, DH)],
            att_send.at[h, r],
            att_recv.at[h, back(r)],
            peer(r),
        )

    def attention_got(h, r):
        ref = abuf.at[h, :, :, pl.ds(r * DH, DH)]
        return remote(ref, ref, att_send.at[h, r], att_recv.at[h, r], peer(r))

    def order(d):
        return ((d, d), (d, 1 - d))

    def begin(h, which):
        for d in range(2):
            ring(d, h, 1, order(d)[which][1]).start()

    def pass_on(h, s):
        for which in range(2):
            for d in range(2):
                p = order(d)[which][1]
                if s == 4 and which == 1:
                    continue
                ring(d, h, s, p).wait_recv()
                if s < 3 or (s == 3 and which == 0):
                    ring(d, h, s + 1, p).start()
                twin(d, h, s, p).start()

    def twins_arrived(h, s):
        for d in range(2):
            for which in range(1 if s == 4 else 2):
                twin_got(d, h, s, order(d)[which][1]).wait_recv()

    def attend(h, slot):
        q = qq[h].reshape(2 * rows, 2 * DH)
        k = kv[slot, h, 0].reshape(2 * rows, 2 * DH)
        v = kv[slot, h, 1].reshape(2 * rows, 2 * DH)
        scores = lax.dot_general(q[:, DH:], k[:, :DH], NT, preferred_element_type=F32)
        score_tan = lax.dot_general(q, k, NT, preferred_element_type=F32)
        old = top[...]
        new = jnp.maximum(old, jnp.max(scores, axis=1, keepdims=True))
        top[...] = new
        alpha = jnp.exp2((old - new) * BASE2)
        weights, mixed = [], []
        for j in range(2 * rows // DH):
            block = slice(j * DH, (j + 1) * DH)
            exponent = jnp.exp2((scores[:, block] - new) * BASE2)
            weights.append(exponent)
            mixed.append(exponent * score_tan[:, block])
        norm[...] = alpha * norm[...] + functools.reduce(jnp.add, weights)
        slope[...] = alpha * slope[...] + functools.reduce(jnp.add, mixed)
        weights = jnp.concatenate([w.astype(BF16) for w in weights], axis=1)
        mixed = jnp.concatenate([w.astype(BF16) for w in mixed], axis=1)
        plain = lax.dot_general(weights, v, NN, preferred_element_type=F32)
        cross = lax.dot_general(mixed, v[:, :DH], NN, preferred_element_type=F32)
        total[0] = alpha * total[0] + plain[:, :DH]
        total[1] = alpha * total[1] + (plain[:, DH:] + FACTOR * cross)

    def finish(h):
        normalizer = jnp.sum(norm[...], axis=1, keepdims=True)
        inverse = 1.0 / normalizer
        slope_mean = FACTOR * jnp.sum(slope[...], axis=1, keepdims=True) * inverse
        plain = total[0] * inverse
        tan = total[1] * inverse - plain * slope_mean
        lse = top[...] * BASE2 + jnp.log2(normalizer)
        own[0] = plain[:rows]
        own[1] = tan[:rows]
        own_lse[...] = lse[:rows]
        own_slope[...] = jnp.broadcast_to(slope_mean[:rows], (rows, DH))
        part[h, 0] = plain[rows:].astype(BF16)
        part[h, 1] = tan[rows:].astype(BF16)
        lane = lax.broadcasted_iota(jnp.int32, (rows, DH), 1)
        both = jnp.where(lane == 0, lse[rows:], slope_mean[rows:])
        both = jnp.concatenate([both, jnp.zeros((256 - rows, DH), F32)], axis=0)
        stat[h] = both.T[:8]
        for copy in part_copies(h):
            copy.start()

    def combine(h):
        for copy in part_copies(h):
            copy.wait_recv()
        both = jnp.concatenate([stat_got[h], jnp.zeros((DH - 8, 256), F32)], axis=0).T
        lse1, slope1 = both[:rows, 0:1], both[:rows, 1:2]
        lse0, slope0 = own_lse[...], own_slope[...]
        most = jnp.maximum(lse0, lse1)
        e0, e1 = jnp.exp2(lse0 - most), jnp.exp2(lse1 - most)
        inverse = 1.0 / (e0 + e1)
        w0, w1 = e0 * inverse, e1 * inverse
        a0, a1 = own[0], part_got[h, 0].astype(F32)
        t0, t1 = own[1], part_got[h, 1].astype(F32)
        abuf[h, 0, :, :DH] = (w0 * a0 + w1 * a1).astype(BF16)
        tan = w0 * t0 + w1 * t1 + (w0 * w1) * (slope0 - slope1) * (a0 - a1)
        abuf[h, 1, :, :DH] = tan.astype(BF16)
        for r in range(1, 2 * WIDE):
            attention_copy(h, r).start()

    def project(h):
        for r in range(1, 2 * WIDE):
            attention_got(h, r).wait_recv()
        left = abuf[h].reshape(2 * rows, 2 * WIDE * DH)
        right = wbuf[h].reshape(2 * WIDE * DH, width)
        acc[...] += lax.dot_general(left, right, NN, preferred_element_type=F32)

    for copy in loads[: 4 * HEADS]:
        copy.wait()
    begin(0, 0)
    begin(0, 1)
    for copy in loads[4 * HEADS : 6 * HEADS]:
        copy.wait()
    query_copy().start()
    for h in range(HEADS):
        first(h, c).start()
    acc[...] = jnp.zeros_like(acc)
    loads[-1].wait()
    weight(1).start()
    weight(4).start()
    pass_on(0, 1)
    query_copy().wait_recv()

    def step(t, carry):
        h, slot = t // RING, t % RING

        @pl.when(slot == 0)
        def _():
            top[...] = jnp.full_like(top, -1e30)
            norm[...] = jnp.zeros_like(norm)
            slope[...] = jnp.zeros_like(slope)
            total[...] = jnp.zeros_like(total)
            first(h, 1 - c).wait_recv()

        @pl.when((slot == 0) & (h < HEADS - 1))
        def _():
            begin(h + 1, 0)

        @pl.when(slot == 1)
        def _():
            pass_on(h, 2)

        @pl.when((slot == 1) & (h < HEADS - 1))
        def _():
            begin(h + 1, 1)

        @pl.when(slot == 1)
        def _():
            twins_arrived(h, 1)

        @pl.when(t == 2)
        def _():
            weight(3).start()
            weight(5).start()

        @pl.when(slot == 3)
        def _():
            twins_arrived(h, 2)

        @pl.when((slot == 4) & (h > 0))
        def _():
            combine(h - 1)

        @pl.when(t == 4)
        def _():
            weight(2).start()
            weight(7).start()

        @pl.when(slot == 5)
        def _():
            pass_on(h, 3)
            twins_arrived(h, 3)

        @pl.when(t == 6)
        def _():
            weight(6).start()

        @pl.when(t == RING + 2)
        def _():
            for r in range(1, 2 * WIDE):
                weight_got(r).wait_recv()
                weight_twin(r, c).start()

        @pl.when((slot == 7) & (h < HEADS - 1))
        def _():
            pass_on(h + 1, 1)

        @pl.when(slot == 7)
        def _():
            pass_on(h, 4)
            twins_arrived(h, 4)

        attend(h, slot)

        @pl.when(slot == 7)
        def _():
            finish(h)

        @pl.when(t == 2 * RING - 1)
        def _():
            for r in range(1, 2 * WIDE):
                weight_twin(r, 1 - c).wait_recv()

        @pl.when((slot == 7) & (h > 0))
        def _():
            project(h - 1)

        return carry

    lax.fori_loop(0, HEADS * RING, step, 0)
    combine(HEADS - 1)
    project(HEADS - 1)

    scale = gate[...]
    projected = acc[:rows]
    update[...] = (scale * projected).astype(BF16)
    update_tan[...] = (gate_tan[...] * projected + scale * acc[rows:]).astype(BF16)

    query_copy().wait_send()

    def drain(h, carry):
        first(h, c).wait_send()
        for copy in part_copies(h):
            copy.wait_send()
        for r in range(1, 2 * WIDE):
            attention_copy(h, r).wait_send()
        for s in range(1, 5):
            for d in range(2):
                for which in range(1 if s == 4 else 2):
                    ring(d, h, s, order(d)[which][1]).wait_send()
                    twin(d, h, s, order(d)[which][1]).wait_send()
        return carry

    lax.fori_loop(0, HEADS, drain, 0)
    for r in range(1, 2 * WIDE):
        weight(r).wait_send()
        weight_twin(r, c).wait_send()


def local(queries, keys, values, query_tan, key_tan, value_tan, out_weight, gate, gate_tan):
    rows = queries.shape[0]
    width = gate.shape[0]
    dma = pltpu.SemaphoreType.DMA
    anywhere = pl.BlockSpec(memory_space=pl.ANY)
    vmem = pl.BlockSpec(memory_space=pltpu.VMEM)
    out = jax.ShapeDtypeStruct((rows, width), BF16)
    return pl.pallas_call(
        functools.partial(kernel, rows, width),
        out_shape=(out, out),
        in_specs=[anywhere] * 7 + [vmem] * 2,
        out_specs=(vmem, vmem),
        scratch_shapes=[
            pltpu.VMEM((HEADS, 2, rows, 2 * DH), BF16),
            pltpu.VMEM((RING, HEADS, 2, 2, rows, 2 * DH), BF16),
            pltpu.VMEM((HEADS, 2 * WIDE, DH, width), BF16),
            pltpu.VMEM((HEADS, 2, rows, 2 * WIDE * DH), BF16),
            pltpu.VMEM((2 * rows, DH), F32),
            pltpu.VMEM((2 * rows, DH), F32),
            pltpu.VMEM((2 * rows, DH), F32),
            pltpu.VMEM((2, 2 * rows, DH), F32),
            pltpu.VMEM((2, rows, DH), F32),
            pltpu.VMEM((rows, DH), F32),
            pltpu.VMEM((rows, DH), F32),
            pltpu.VMEM((HEADS, 2, rows, DH), BF16),
            pltpu.VMEM((HEADS, 2, rows, DH), BF16),
            pltpu.VMEM((HEADS, 8, 256), F32),
            pltpu.VMEM((HEADS, 8, 256), F32),
            pltpu.VMEM((2 * rows, width), F32),
            dma((6 * HEADS + 1,)),
            dma((2,)),
            dma((2, HEADS, 7)),
            dma((2, HEADS, 7)),
            dma((2, HEADS, 7)),
            dma((2, HEADS, 7)),
            dma((2, HEADS)),
            dma((2 * WIDE,)),
            dma((2 * WIDE,)),
            dma((2 * WIDE,)),
            dma((2 * WIDE,)),
            dma((2, HEADS, 2)),
            dma((HEADS, 2 * WIDE)),
            dma((HEADS, 2 * WIDE)),
        ],
        compiler_params=pltpu.CompilerParams(
            collective_id=0, has_side_effects=True, vmem_limit_bytes=48 << 20
        ),
    )(
        queries,
        keys,
        values,
        query_tan,
        key_tan,
        value_tan,
        out_weight.reshape(HEADS, DH, -1),
        gate.reshape(1, -1),
        gate_tan.reshape(1, -1),
    )


def solution(mesh):
    token = P("ctx", "head")
    in_specs = (token,) * 6 + (P("head", None), P("head"), P("head"))
    return jax.shard_map(
        local, mesh=mesh, in_specs=in_specs, out_specs=(token, token), check_vma=False
    )
```

time: 485 us -> 108 us (0.22)
  waiting for transfers between devices: 296 us -> 0 us
  Pallas kernels: 0 us -> 96.9 us
  matrix products: 79.6 us -> 0 us
  local copies, waits for them, and re-layouts: 85.6 us -> 10.3 us
  between operations: 13.9 us -> 0.65 us
    all_gather x4 -> x0, waiting for transfers between devices: 207 us -> none  [the longest x1 70.1 us: local(): lax.all_gather(keys, 'ctx', axis=0, tiled=True)]
    pallas_call x0 -> x1, Pallas kernels: none -> 96.9 us  [local(): pl.pallas_call(functools.partial(kernel, rows, width), out_shape=(out, ou...]
    unnamed x6 -> x0, waiting for transfers between devices: 89.4 us -> none
    dot_general x43 -> x0, matrix products: 79.6 us -> none  [the longest x12 19.8 us: plain_scores(): jnp.einsum('hqd,khd->hqk', query_heads, key_block, preferred_element_type...]
    reshape x7 -> x2, local copies, waits for them, and re-layouts: 53.7 us -> 1.38 us  [the longest x1 0.69 us: local(): gate.reshape(1, -1)]
    unnamed x12 -> x16, local copies, waits for them, and re-layouts: 31.9 us -> 8.96 us
  transfers between devices with their start and end apart: 5 -> 0, of which waited for: 5 -> 0; matrix products, arithmetic and copies ran while one was open for 15% -> 0% of each run, Pallas kernels for 0% -> 0%
where the time goes in v1:
time: 108 us
  Pallas kernels  96.9 us (90%)
  local copies, waits for them, and re-layouts  10.3 us (10%)
    pallas_call x1, Pallas kernels, local(): pl.pallas_call(functools.partial(kernel, rows, width), out_shape=(out, ou...  96.9 us
    unnamed x16, local copies, waits for them, and re-layouts  8.96 us

profile of v1, /device:TPU:1, one launch (start us, length us, event | category | flops | bytes accessed | tf_op | source)
XLA Modules:
  0.0 107.8 jit_solution(507131960800624449)
XLA Ops:
  0.6 0.7 reshape.14.gate
  1.3 0.7 reshape.15.gate_tan
  2.0 0.0 copy-start
  2.0 2.1 %copy-done = bf16[384,5120]{1,0:T(8,128)(2,1)S(1)} copy-done((bf16[384,5120]{1,0:T(8,128)(2,1)S(1)}, bf16[384,5120]{1,0:T(8,128)(2,1)}, u32[]{:S(2)}) %copy-start) | copy-done | bytes 3932184
  4.1 0.0 copy-start.1
  4.1 0.9 copy-done.1
  5.0 0.0 copy-start.2
  5.0 0.9 copy-done.2
  5.9 0.0 copy-start.3
  5.9 0.9 copy-done.3
  6.9 0.0 copy-start.4
  6.9 0.9 copy-done.4
  7.8 0.0 copy-start.5
  7.8 0.9 copy-done.5
  8.7 0.0 copy-start.6
  8.7 0.9 copy-done.6
  9.6 96.9 %shard_map.104 = (bf16[192,640]{1,0:T(8,128)(2,1)S(1)}, bf16[192,640]{1,0:T(8,128)(2,1)S(1)}) custom-call(bf16[192,384]{1,0:T(8,128)(2,1)S(1)} %copy-done.1, bf16[192,384]{1,0:T(8,128)(2,1)S(1)} %copy-done.2, bf16[192,384]{1,0:T(8,128)(2,1)S(1)} %copy-done.3, bf16[192,384]{1,0:T(8,128)(2,1)S(1)} %copy-done.4, bf16[192,384]{1,0:T(8,128)(2,1)S(1)} %copy-done.5, ...), custom_call_target="tpu_custom_call" | custom-call | tf_op jit(solution)/shard_map/pallas_call | solution.py:424
  106.5 0.7 copy.13
  107.2 0.7 copy.14
Async XLA Ops:
  2.0 2.1 %copy-start = (bf16[384,5120]{1,0:T(8,128)(2,1)S(1)}, bf16[384,5120]{1,0:T(8,128)(2,1)}, u32[]{:S(2)}) copy-start(bf16[384,5120]{1,0:T(8,128)(2,1)} %param.15) | copy-start | bytes 11796484
  4.1 0.9 copy-start.1
  5.0 0.9 copy-start.2
  5.9 0.9 copy-start.3
  6.9 0.9 copy-start.4
  7.8 0.9 copy-start.5
  8.7 0.9 copy-start.6

commit v2 on v1

--- a/solution.py
+++ b/solution.py
@@ -31,10 +31,7 @@
     key_tan,
     value_tan,
     out_weight,
-    gate,
-    gate_tan,
-    update,
-    update_tan,
+    acc,
     qq,
     kv,
     wbuf,
@@ -50,7 +47,6 @@
     part_got,
     stat,
     stat_got,
-    acc,
     load_sem,
     q_sem,
     ring_send,
@@ -293,8 +289,8 @@
         first(h, c).start()
     acc[...] = jnp.zeros_like(acc)
     loads[-1].wait()
-    weight(1).start()
-    weight(4).start()
+    for r in range(1, 2 * WIDE):
+        weight(r).start()
     pass_on(0, 1)
     query_copy().wait_recv()
 
@@ -325,39 +321,31 @@
         def _():
             twins_arrived(h, 1)
 
-        @pl.when(t == 2)
-        def _():
-            weight(3).start()
-            weight(5).start()
+        @pl.when((slot == 3) & (h > 0))
+        def _():
+            combine(h - 1)
 
         @pl.when(slot == 3)
         def _():
             twins_arrived(h, 2)
-
-        @pl.when((slot == 4) & (h > 0))
-        def _():
-            combine(h - 1)
-
-        @pl.when(t == 4)
-        def _():
-            weight(2).start()
-            weight(7).start()
 
         @pl.when(slot == 5)
         def _():
             pass_on(h, 3)
             twins_arrived(h, 3)
 
-        @pl.when(t == 6)
-        def _():
-            weight(6).start()
-
-        @pl.when(t == RING + 2)
+        @pl.when(t == 2 * RING - 2)
         def _():
             for r in range(1, 2 * WIDE):
                 weight_got(r).wait_recv()
                 weight_twin(r, c).start()
 
+        @pl.when(t == 3 * RING - 2)
+        def _():
+            for r in range(1, 2 * WIDE):
+                weight_twin(r, 1 - c).wait_recv()
+            project(0)
+
         @pl.when((slot == 7) & (h < HEADS - 1))
         def _():
             pass_on(h + 1, 1)
@@ -373,25 +361,12 @@
         def _():
             finish(h)
 
-        @pl.when(t == 2 * RING - 1)
-        def _():
-            for r in range(1, 2 * WIDE):
-                weight_twin(r, 1 - c).wait_recv()
-
-        @pl.when((slot == 7) & (h > 0))
-        def _():
-            project(h - 1)
-
         return carry
 
     lax.fori_loop(0, HEADS * RING, step, 0)
+    project(HEADS - 2)
     combine(HEADS - 1)
     project(HEADS - 1)
-
-    scale = gate[...]
-    projected = acc[:rows]
-    update[...] = (scale * projected).astype(BF16)
-    update_tan[...] = (gate_tan[...] * projected + scale * acc[rows:]).astype(BF16)
 
     query_copy().wait_send()
 
@@ -415,17 +390,18 @@
 
 
 def local(queries, keys, values, query_tan, key_tan, value_tan, out_weight, gate, gate_tan):
+    fixed = (queries, keys, values, query_tan, key_tan, value_tan, out_weight.reshape(HEADS, DH, -1))
+    fixed = [pltpu.with_memory_space_constraint(array, pltpu.HBM) for array in fixed]
     rows = queries.shape[0]
     width = gate.shape[0]
     dma = pltpu.SemaphoreType.DMA
-    anywhere = pl.BlockSpec(memory_space=pl.ANY)
+    hbm = pl.BlockSpec(memory_space=pltpu.HBM)
     vmem = pl.BlockSpec(memory_space=pltpu.VMEM)
-    out = jax.ShapeDtypeStruct((rows, width), BF16)
-    return pl.pallas_call(
+    projected = pl.pallas_call(
         functools.partial(kernel, rows, width),
-        out_shape=(out, out),
-        in_specs=[anywhere] * 7 + [vmem] * 2,
-        out_specs=(vmem, vmem),
+        out_shape=jax.ShapeDtypeStruct((2 * rows, width), F32),
+        in_specs=[hbm] * 7,
+        out_specs=vmem,
         scratch_shapes=[
             pltpu.VMEM((HEADS, 2, rows, 2 * DH), BF16),
             pltpu.VMEM((RING, HEADS, 2, 2, rows, 2 * DH), BF16),
@@ -442,7 +418,6 @@
             pltpu.VMEM((HEADS, 2, rows, DH), BF16),
             pltpu.VMEM((HEADS, 8, 256), F32),
             pltpu.VMEM((HEADS, 8, 256), F32),
-            pltpu.VMEM((2 * rows, width), F32),
             dma((6 * HEADS + 1,)),
             dma((2,)),
             dma((2, HEADS, 7)),
@@ -459,19 +434,13 @@
             dma((HEADS, 2 * WIDE)),
         ],
         compiler_params=pltpu.CompilerParams(
-            collective_id=0, has_side_effects=True, vmem_limit_bytes=48 << 20
+            collective_id=0, has_side_effects=True, vmem_limit_bytes=40 << 20
         ),
-    )(
-        queries,
-        keys,
-        values,
-        query_tan,
-        key_tan,
-        value_tan,
-        out_weight.reshape(HEADS, DH, -1),
-        gate.reshape(1, -1),
-        gate_tan.reshape(1, -1),
-    )
+    )(*fixed)
+    plain, tan = projected[:rows], projected[rows:]
+    update = (gate[None, :] * plain).astype(BF16)
+    update_tan = (gate_tan[None, :] * plain + gate[None, :] * tan).astype(BF16)
+    return update, update_tan
 
 
 def solution(mesh):

time: 108 us -> 91.3 us (0.85)
  local copies, waits for them, and re-layouts: 10.3 us -> 0.01 us
  Pallas kernels: 96.9 us -> 89.6 us
    unnamed x16 -> x4, local copies, waits for them, and re-layouts: 8.96 us -> 0.01 us
    pallas_call x1, Pallas kernels: 96.9 us -> 89.6 us  [local(): pl.pallas_call(functools.partial(kernel, rows, width), out_shape=jax.Shap...]
    reshape x2 -> x0, local copies, waits for them, and re-layouts: 1.38 us -> none  [the longest x1 0.69 us: local(): gate.reshape(1, -1)]
where the time goes in v2:
time: 91.3 us; the launch traced here: 91.2 us
  Pallas kernels  89.6 us (98%)
    pallas_call x1, Pallas kernels, local(): pl.pallas_call(functools.partial(kernel, rows, width), out_shape=jax.Shap...  89.6 us

profile of v2, /device:TPU:1, one launch (start us, length us, event | category | flops | bytes accessed | tf_op | source)
XLA Modules:
  0.0 91.2 jit_solution(5482976033587000760)
XLA Ops:
  0.6 0.0 copy-start
  0.6 0.0 copy-start.1
  0.7 89.6 %shard_map.104 = f32[384,640]{1,0:T(8,128)S(1)} custom-call(bf16[192,384]{1,0:T(8,128)(2,1)} %queries.1, bf16[192,384]{1,0:T(8,128)(2,1)} %keys.1, bf16[192,384]{1,0:T(8,128)(2,1)} %values.1, bf16[192,384]{1,0:T(8,128)(2,1)} %query_tan.1, bf16[192,384]{1,0:T(8,128)(2,1)} %key_tan.1, bf16[192,384]{1,0:T(8,128)(2,1)} %value_tan.1, bf16[3,128,5120]{2,1,0:T(8,128)(2,1)} %bitcast.1), custom_call_target="tpu_custom_call" | custom-call | tf_op jit(solution)/shard_map/pallas_call | solution.py:400
  90.3 0.0 copy-done
  90.3 0.0 copy-done.1
  90.3 0.9 add_convert_fusion
Async XLA Ops:
  0.6 89.7 %copy-start = (f32[640]{0:T(1024)S(1)}, f32[640]{0:T(1024)}, u32[]{:S(2)}) copy-start(f32[640]{0:T(1024)} %param.17) | copy-start | bytes 7684
  0.6 89.7 %copy-start.1 = (f32[640]{0:T(1024)S(1)}, f32[640]{0:T(1024)}, u32[]{:S(2)}) copy-start(f32[640]{0:T(1024)} %param.16) | copy-start | bytes 7684

commit v3 on v2

--- a/solution.py
+++ b/solution.py
@@ -78,6 +78,11 @@
     def back(r):
         return (r // WIDE) * WIDE + (WIDE - r % WIDE) % WIDE
 
+    barrier = pltpu.get_barrier_semaphore()
+    others = [ahead, behind, sibling, partner] + [peer(r) for r in range(1, 2 * WIDE)]
+    for other in others:
+        pl.semaphore_signal(barrier, inc=1, device_id=other, device_id_type=MESH)
+
     loads = []
 
     def load(src, dst):
@@ -97,10 +102,6 @@
         load(queries.at[:, cols(h)], qq.at[h, 0, :, pl.ds(DH, DH)])
     load(out_weight.at[:, :, pl.ds(pl.multiple_of(g * width, 128), width)], wbuf.at[:, 0])
 
-    barrier = pltpu.get_barrier_semaphore()
-    others = [ahead, behind, sibling, partner] + [peer(r) for r in range(1, 2 * WIDE)]
-    for other in others:
-        pl.semaphore_signal(barrier, inc=1, device_id=other, device_id_type=MESH)
     pl.semaphore_wait(barrier, len(others))
 
     def remote(src, dst, send, recv, device):
@@ -172,13 +173,17 @@
             remote(stat.at[h], stat_got.at[h], part_sem.at[0, h, 1], part_sem.at[1, h, 1], partner),
         )
 
-    def attention_copy(h, r):
+    straight = ((0, 4, 4), (0, 2, 2), (0, 1, 3), (0, 3, 1))
+    onward = ((4, 1, 7), (4, 3, 5), (2, 4, 6))
+
+    def attention_copy(h, leg):
+        source, target, lands = leg
         return remote(
-            abuf.at[h, :, :, pl.ds(0, DH)],
-            abuf.at[h, :, :, pl.ds(back(r) * DH, DH)],
-            att_send.at[h, r],
-            att_recv.at[h, back(r)],
-            peer(r),
+            abuf.at[h, :, :, pl.ds(source * DH, DH)],
+            abuf.at[h, :, :, pl.ds(lands * DH, DH)],
+            att_send.at[h, lands],
+            att_recv.at[h, lands],
+            peer(target),
         )
 
     def attention_got(h, r):
@@ -268,14 +273,22 @@
         abuf[h, 0, :, :DH] = (w0 * a0 + w1 * a1).astype(BF16)
         tan = w0 * t0 + w1 * t1 + (w0 * w1) * (slope0 - slope1) * (a0 - a1)
         abuf[h, 1, :, :DH] = tan.astype(BF16)
-        for r in range(1, 2 * WIDE):
-            attention_copy(h, r).start()
-
-    def project(h):
-        for r in range(1, 2 * WIDE):
-            attention_got(h, r).wait_recv()
-        left = abuf[h].reshape(2 * rows, 2 * WIDE * DH)
-        right = wbuf[h].reshape(2 * WIDE * DH, width)
+        for leg in straight:
+            attention_copy(h, leg).start()
+
+    def hand_on(h):
+        attention_got(h, 4).wait_recv()
+        for leg in onward[:2]:
+            attention_copy(h, leg).start()
+        attention_got(h, 2).wait_recv()
+        attention_copy(h, onward[2]).start()
+
+    def project(h, low, high):
+        for r in range(low, high):
+            if r not in (0, 2, 4):
+                attention_got(h, r).wait_recv()
+        left = abuf[h, :, :, low * DH : high * DH].reshape(2 * rows, (high - low) * DH)
+        right = wbuf[h, low:high].reshape((high - low) * DH, width)
         acc[...] += lax.dot_general(left, right, NN, preferred_element_type=F32)
 
     for copy in loads[: 4 * HEADS]:
@@ -289,8 +302,6 @@
         first(h, c).start()
     acc[...] = jnp.zeros_like(acc)
     loads[-1].wait()
-    for r in range(1, 2 * WIDE):
-        weight(r).start()
     pass_on(0, 1)
     query_copy().wait_recv()
 
@@ -321,9 +332,15 @@
         def _():
             twins_arrived(h, 1)
 
-        @pl.when((slot == 3) & (h > 0))
-        def _():
-            combine(h - 1)
+        for r, when in ((6, 0), (5, 1), (7, 2), (4, 3), (2, 4), (1, 5), (3, 6)):
+
+            @pl.when(t == when)
+            def _():
+                weight(r).start()
+
+        @pl.when(t == 2 * RING + 3)
+        def _():
+            combine(1)
 
         @pl.when(slot == 3)
         def _():
@@ -334,17 +351,23 @@
             pass_on(h, 3)
             twins_arrived(h, 3)
 
-        @pl.when(t == 2 * RING - 2)
+        @pl.when(t == RING + 5)
+        def _():
+            combine(0)
+
+        @pl.when(t == 2 * RING + 2)
         def _():
             for r in range(1, 2 * WIDE):
                 weight_got(r).wait_recv()
                 weight_twin(r, c).start()
 
+        @pl.when(t == 2 * RING + 1)
+        def _():
+            hand_on(0)
+
         @pl.when(t == 3 * RING - 2)
         def _():
-            for r in range(1, 2 * WIDE):
-                weight_twin(r, 1 - c).wait_recv()
-            project(0)
+            hand_on(1)
 
         @pl.when((slot == 7) & (h < HEADS - 1))
         def _():
@@ -364,9 +387,14 @@
         return carry
 
     lax.fori_loop(0, HEADS * RING, step, 0)
-    project(HEADS - 2)
-    combine(HEADS - 1)
-    project(HEADS - 1)
+    for r in range(1, 2 * WIDE):
+        weight_twin(r, 1 - c).wait_recv()
+    project(0, 0, 2 * WIDE)
+    combine(2)
+    project(1, 0, 2 * WIDE)
+    hand_on(2)
+    project(2, 0, 5)
+    project(2, 5, 2 * WIDE)
 
     query_copy().wait_send()
 
@@ -374,8 +402,8 @@
         first(h, c).wait_send()
         for copy in part_copies(h):
             copy.wait_send()
-        for r in range(1, 2 * WIDE):
-            attention_copy(h, r).wait_send()
+        for leg in straight + onward:
+            attention_copy(h, leg).wait_send()
         for s in range(1, 5):
             for d in range(2):
                 for which in range(1 if s == 4 else 2):

time: 91.3 us -> 82.5 us (0.904)
  Pallas kernels: 89.6 us -> 80.8 us
    pallas_call x1, Pallas kernels: 89.6 us -> 80.8 us  [local(): pl.pallas_call(functools.partial(kernel, rows, width), out_shape=jax.Shap...]
where the time goes in v3:
time: 82.5 us; the launch traced here: 82.4 us
  Pallas kernels  80.8 us (98%)
  other arithmetic  0.87 us (1%)
    pallas_call x1, Pallas kernels, local(): pl.pallas_call(functools.partial(kernel, rows, width), out_shape=jax.Shap...  80.8 us

profile of v3, /device:TPU:1, one launch (start us, length us, event | category | flops | bytes accessed | tf_op | source)
XLA Modules:
  0.0 82.4 jit_solution(6300135755962132574)
XLA Ops:
  0.6 0.0 copy-start
  0.6 0.0 copy-start.1
  0.7 80.8 %shard_map.104 = f32[384,640]{1,0:T(8,128)S(1)} custom-call(bf16[192,384]{1,0:T(8,128)(2,1)} %queries.1, bf16[192,384]{1,0:T(8,128)(2,1)} %keys.1, bf16[192,384]{1,0:T(8,128)(2,1)} %values.1, bf16[192,384]{1,0:T(8,128)(2,1)} %query_tan.1, bf16[192,384]{1,0:T(8,128)(2,1)} %key_tan.1, bf16[192,384]{1,0:T(8,128)(2,1)} %value_tan.1, bf16[3,128,5120]{2,1,0:T(8,128)(2,1)} %bitcast.1), custom_call_target="tpu_custom_call" | custom-call | tf_op jit(solution)/shard_map/pallas_call | solution.py:428
  81.5 0.0 copy-done
  81.5 0.0 copy-done.1
  81.5 0.9 %add_convert_fusion = (bf16[192,640]{1,0:T(8,128)(2,1)}, bf16[192,640]{1,0:T(8,128)(2,1)}) fusion(f32[384,640]{1,0:T(8,128)S(1)} %shard_map.104, f32[640]{0:T(1024)S(1)} %copy-done, f32[640]{0:T(1024)S(1)} %copy-done.1), kind=kLoop, calls=%fused_computation | loop fusion | flops 737280 | bytes 1479680 | tf_op jit(solution)/shard_map/convert_element_type | solution.py:470
Async XLA Ops:
  0.6 80.9 %copy-start = (f32[640]{0:T(1024)S(1)}, f32[640]{0:T(1024)}, u32[]{:S(2)}) copy-start(f32[640]{0:T(1024)} %param.17) | copy-start | bytes 7684
  0.6 80.9 %copy-start.1 = (f32[640]{0:T(1024)S(1)}, f32[640]{0:T(1024)}, u32[]{:S(2)}) copy-start(f32[640]{0:T(1024)} %param.16) | copy-start | bytes 7684

commit v4 on v3

v4 whole, which is shorter than its diff:
```python
import functools
import math

import jax
import jax.numpy as jnp
from jax import lax
from jax.experimental import pallas as pl
from jax.experimental.pallas import tpu as pltpu
from jax.sharding import PartitionSpec as P

DH = 128
HEADS = 3
RING = 8
WIDE = 4
FACTOR = 1.0 / math.sqrt(DH)
BASE2 = FACTOR * math.log2(math.e)
MESH = pl.DeviceIdType.MESH
F32 = jnp.float32
BF16 = jnp.bfloat16
NT = (((1,), (1,)), ((), ()))
NN = (((1,), (0,)), ((), ()))
SEND, TAKE = 0, 1
JOIN, PASS = 2, 3
PLAN = (
    ((SEND, 0, 1, 0), (SEND, 0, 1, 1), (SEND, 1, 1, 0), (TAKE, 0, 1, 0), (SEND, 0, 2, 0), (TAKE, 0, 1, 1), (SEND, 0, 2, 1), (SEND, 1, 1, 1)),
    ((TAKE, 1, 1, 0),),
    (),
    ((TAKE, 0, 2, 0), (SEND, 0, 3, 0), (SEND, 1, 2, 0), (TAKE, 0, 2, 1), (SEND, 0, 3, 1), (TAKE, 1, 1, 1)),
    (),
    ((TAKE, 0, 3, 0), (SEND, 0, 4, 0), (SEND, 1, 2, 1), (SEND, 2, 1, 0), (TAKE, 1, 2, 0), (SEND, 1, 3, 0), (SEND, 2, 1, 1), (TAKE, 0, 3, 1), (TAKE, 0, 4, 0)),
    (),
    ((TAKE, 1, 2, 1), (SEND, 1, 3, 1)),
    (),
    (),
    ((TAKE, 2, 1, 0), (SEND, 2, 2, 0)),
    (),
    (),
    ((TAKE, 1, 3, 0), (SEND, 1, 4, 0), (JOIN, 0), (TAKE, 2, 1, 1), (SEND, 2, 2, 1), (TAKE, 1, 3, 1), (TAKE, 2, 2, 0), (SEND, 2, 3, 0)),
    (),
    ((TAKE, 1, 4, 0), (TAKE, 2, 2, 1), (SEND, 2, 3, 1)),
    ((PASS, 0),),
    ((TAKE, 2, 3, 0), (SEND, 2, 4, 0)),
    (),
    (),
    (),
    ((TAKE, 2, 3, 1), (JOIN, 1), (TAKE, 2, 4, 0)),
    (),
    (),
)


def kernel(
    rows,
    width,
    queries,
    keys,
    values,
    query_tan,
    key_tan,
    value_tan,
    out_weight,
    acc,
    qq,
    kv,
    wbuf,
    abuf,
    top,
    norm,
    slope,
    total,
    own,
    own_lse,
    own_slope,
    part,
    part_got,
    stat,
    stat_got,
    load_sem,
    q_sem,
    ring_send,
    ring_recv,
    sib_send,
    sib_recv,
    first_sem,
    w_send,
    w_recv,
    w_sib_send,
    w_sib_recv,
    part_sem,
    att_send,
    att_recv,
):
    half = rows // 2
    i = lax.axis_index("ctx")
    g = lax.axis_index("head")
    z, y, c = i // 4, (i // 2) % 2, i % 2
    yh, x = g // WIDE, g % WIDE
    ahead = (((z + 1) % RING) * 4 + y * 2 + c, g)
    behind = (((z + RING - 1) % RING) * 4 + y * 2 + c, g)
    sibling = (z * 4 + y * 2 + 1 - c, g)
    partner = (z * 4 + (1 - y) * 2 + c, g)

    def peer(r):
        return (i, ((yh + r // WIDE) % 2) * WIDE + (x + r % WIDE) % WIDE)

    def back(r):
        return (r // WIDE) * WIDE + (WIDE - r % WIDE) % WIDE

    barrier = pltpu.get_barrier_semaphore()
    others = [ahead, behind, sibling, partner] + [peer(r) for r in range(1, 2 * WIDE)]
    for other in others:
        pl.semaphore_signal(barrier, inc=1, device_id=other, device_id_type=MESH)

    loads = []

    def load(src, dst):
        copy = pltpu.make_async_copy(src, dst, load_sem.at[len(loads)])
        copy.start()
        loads.append(copy)

    def cols(h):
        return pl.ds(h * DH, DH)

    def load_keys(h):
        for pair, low, high in ((0, keys, key_tan), (1, values, value_tan)):
            load(low.at[:, cols(h)], kv.at[0, h, pair, c, :, pl.ds(0, DH)])
            load(high.at[:, cols(h)], kv.at[0, h, pair, c, :, pl.ds(DH, DH)])

    load_keys(0)
    for h in range(HEADS):
        load(query_tan.at[:, cols(h)], qq.at[h, 0, :, pl.ds(0, DH)])
        load(queries.at[:, cols(h)], qq.at[h, 0, :, pl.ds(DH, DH)])
    load_keys(1)
    load_keys(2)
    load(out_weight.at[:, :, pl.ds(pl.multiple_of(g * width, 128), width)], wbuf.at[:, 0])

    pl.semaphore_wait(barrier, len(others))

    def remote(src, dst, send, recv, device):
        return pltpu.make_async_remote_copy(
            src_ref=src,
            dst_ref=dst,
            send_sem=send,
            recv_sem=recv,
            device_id=device,
            device_id_type=MESH,
        )

    def slot_of(d, s):
        return 0 if s == 0 else (7 if s == 4 else 2 * s - 1 + d)

    def piece(d, h, s, part_index):
        return kv.at[slot_of(d, s), h, :, c, pl.ds(part_index * half, half)]

    def ring(d, h, s, p):
        tag = 2 * (s - 1) + (p if s < 4 else 0)
        return remote(
            piece(d, h, s - 1, p),
            piece(d, h, s, p),
            ring_send.at[d, h, tag],
            ring_recv.at[d, h, tag],
            ahead if d == 0 else behind,
        )

    def twin(d, h, s, p):
        tag = 2 * (s - 1) + (p if s < 4 else 0)
        ref = piece(d, h, s, p)
        return remote(ref, ref, sib_send.at[d, h, tag], sib_recv.at[d, h, tag], sibling)

    def twin_got(d, h, s, p):
        tag = 2 * (s - 1) + (p if s < 4 else 0)
        ref = kv.at[slot_of(d, s), h, :, 1 - c, pl.ds(p * half, half)]
        return remote(ref, ref, sib_send.at[d, h, tag], sib_recv.at[d, h, tag], sibling)

    def first(h, core):
        ref = kv.at[0, h, :, core]
        return remote(ref, ref, first_sem.at[0, h], first_sem.at[1, h], sibling)

    def query_copy():
        return remote(qq.at[:, 0], qq.at[:, 1], q_sem.at[0], q_sem.at[1], partner)

    share = DH // 2

    def weight(r):
        column = peer(r)[1] * width
        return remote(
            out_weight.at[:, pl.ds(c * share, share), pl.ds(pl.multiple_of(column, 128), width)],
            wbuf.at[:, back(r), pl.ds(c * share, share)],
            w_send.at[r],
            w_recv.at[back(r)],
            peer(r),
        )

    def weight_got(r):
        ref = wbuf.at[:, r, pl.ds(c * share, share)]
        return remote(ref, ref, w_send.at[r], w_recv.at[r], peer(r))

    def weight_twin(r, core):
        ref = wbuf.at[:, r, pl.ds(core * share, share)]
        return remote(ref, ref, w_sib_send.at[r], w_sib_recv.at[r], sibling)

    def part_copies(h, p):
        return (
            remote(
                part.at[h, :, pl.ds(p * half, half)],
                part_got.at[h, :, pl.ds(p * half, half)],
                part_sem.at[0, h, p, 0],
                part_sem.at[1, h, p, 0],
                partner,
            ),
            remote(
                stat.at[h, p],
                stat_got.at[h, p],
                part_sem.at[0, h, p, 1],
                part_sem.at[1, h, p, 1],
                partner,
            ),
        )

    straight = ((0, 4, 4), (0, 2, 2), (0, 1, 3), (0, 3, 1))
    onward = ((4, 1, 7), (4, 3, 5), (2, 4, 6))

    def attention_copy(h, leg, p):
        source, target, lands = leg
        lines = pl.ds(p * half, half)
        return remote(
            abuf.at[h, :, lines, pl.ds(source * DH, DH)],
            abuf.at[h, :, lines, pl.ds(lands * DH, DH)],
            att_send.at[h, lands, p],
            att_recv.at[h, lands, p],
            peer(target),
        )

    def attention_got(h, r, p):
        ref = abuf.at[h, :, pl.ds(p * half, half), pl.ds(r * DH, DH)]
        return remote(ref, ref, att_send.at[h, r, p], att_recv.at[h, r, p], peer(r))

    def order(d):
        return ((d, d), (d, 1 - d))

    def ring_ops(ops):
        waiting = []
        for what, h, *rest in ops:
            if what in (JOIN, PASS):
                for p in range(2):
                    (combine if what == JOIN else hand_on)(h, p)
                continue
            s, which = rest
            if what == TAKE:
                for copy in waiting:
                    copy.start()
                for d in range(2):
                    ring(d, h, s, order(d)[which][1]).wait_recv()
                waiting = [twin(d, h, s, order(d)[which][1]) for d in range(2)]
            else:
                for d in range(2):
                    ring(d, h, s, order(d)[which][1]).start()
        for copy in waiting:
            copy.start()

    def twins_arrived(h, s):
        for d in range(2):
            for which in range(1 if s == 4 else 2):
                twin_got(d, h, s, order(d)[which][1]).wait_recv()

    def attend(h, slot, low=0, high=2):
        lines = slice(low * rows, high * rows)
        q = qq[h, low:high].reshape((high - low) * rows, 2 * DH)
        k = kv[slot, h, 0].reshape(2 * rows, 2 * DH)
        v = kv[slot, h, 1].reshape(2 * rows, 2 * DH)
        scores = lax.dot_general(q[:, DH:], k[:, :DH], NT, preferred_element_type=F32)
        score_tan = lax.dot_general(q, k, NT, preferred_element_type=F32)
        old = top[lines]
        new = jnp.maximum(old, jnp.max(scores, axis=1, keepdims=True))
        top[lines] = new
        alpha = jnp.exp2((old - new) * BASE2)
        weights, mixed = [], []
        for j in range(2 * rows // DH):
            block = slice(j * DH, (j + 1) * DH)
            exponent = jnp.exp2((scores[:, block] - new) * BASE2)
            weights.append(exponent)
            mixed.append(exponent * score_tan[:, block])
        norm[lines] = alpha * norm[lines] + functools.reduce(jnp.add, weights)
        slope[lines] = alpha * slope[lines] + functools.reduce(jnp.add, mixed)
        weights = jnp.concatenate([w.astype(BF16) for w in weights], axis=1)
        mixed = jnp.concatenate([w.astype(BF16) for w in mixed], axis=1)
        plain = lax.dot_general(weights, v, NN, preferred_element_type=F32)
        cross = lax.dot_general(mixed, v[:, :DH], NN, preferred_element_type=F32)
        total[0, lines] = alpha * total[0, lines] + plain[:, :DH]
        total[1, lines] = alpha * total[1, lines] + (plain[:, DH:] + FACTOR * cross)

    def close(low, high):
        lines = slice(low, high)
        normalizer = jnp.sum(norm[lines], axis=1, keepdims=True)
        inverse = 1.0 / normalizer
        slope_mean = FACTOR * jnp.sum(slope[lines], axis=1, keepdims=True) * inverse
        plain = total[0, lines] * inverse
        tan = total[1, lines] * inverse - plain * slope_mean
        return plain, tan, top[lines] * BASE2 + jnp.log2(normalizer), slope_mean

    def finish_partner(h):
        for p in range(2):
            plain, tan, lse, slope_mean = close(rows + p * half, rows + (p + 1) * half)
            part[h, 0, p * half : (p + 1) * half] = plain.astype(BF16)
            part[h, 1, p * half : (p + 1) * half] = tan.astype(BF16)
            lane = lax.broadcasted_iota(jnp.int32, (half, DH), 1)
            both = jnp.where(lane == 0, lse, slope_mean)
            both = jnp.concatenate([both, jnp.zeros((DH - half, DH), F32)], axis=0)
            stat[h, p] = both.T[:8]
            for copy in part_copies(h, p):
                copy.start()

    def finish_own():
        plain, tan, lse, slope_mean = close(0, rows)
        own[0] = plain
        own[1] = tan
        own_lse[...] = lse
        own_slope[...] = jnp.broadcast_to(slope_mean, (rows, DH))

    def combine(h, p):
        for copy in part_copies(h, p):
            copy.wait_recv()
        lines = slice(p * half, (p + 1) * half)
        both = jnp.concatenate([stat_got[h, p], jnp.zeros((DH - 8, DH), F32)], axis=0).T
        lse1, slope1 = both[:half, 0:1], both[:half, 1:2]
        lse0, slope0 = own_lse[lines], own_slope[lines]
        most = jnp.maximum(lse0, lse1)
        e0, e1 = jnp.exp2(lse0 - most), jnp.exp2(lse1 - most)
        inverse = 1.0 / (e0 + e1)
        w0, w1 = e0 * inverse, e1 * inverse
        a0, a1 = own[0, lines], part_got[h, 0, lines].astype(F32)
        t0, t1 = own[1, lines], part_got[h, 1, lines].astype(F32)
        abuf[h, 0, lines, :DH] = (w0 * a0 + w1 * a1).astype(BF16)
        tan = w0 * t0 + w1 * t1 + (w0 * w1) * (slope0 - slope1) * (a0 - a1)
        abuf[h, 1, lines, :DH] = tan.astype(BF16)
        for leg in straight:
            attention_copy(h, leg, p).start()

    def hand_on(h, p):
        attention_got(h, 4, p).wait_recv()
        for leg in onward[:2]:
            attention_copy(h, leg, p).start()
        attention_got(h, 2, p).wait_recv()
        attention_copy(h, onward[2], p).start()

    def project(h, low, high):
        for r in range(low, high):
            if r not in (0, 2, 4):
                for p in range(2):
                    attention_got(h, r, p).wait_recv()
        left = abuf[h, :, :, low * DH : high * DH].reshape(2 * rows, (high - low) * DH)
        right = wbuf[h, low:high].reshape((high - low) * DH, width)
        product = lax.dot_general(left, right, NN, preferred_element_type=F32)
        acc[...] = product if h == 0 else acc[...] + product

    def drain_ring(h):
        first(h, c).wait_send()
        for s in range(1, 5):
            for d in range(2):
                for which in range(1 if s == 4 else 2):
                    ring(d, h, s, order(d)[which][1]).wait_send()
                    twin(d, h, s, order(d)[which][1]).wait_send()

    def drain_weights():
        for r in range(1, 2 * WIDE):
            weight(r).wait_send()
            weight_twin(r, c).wait_send()

    def drain_gather(h, p):
        for leg in straight + onward:
            attention_copy(h, leg, p).wait_send()

    def drain_part(h, p):
        for copy in part_copies(h, p):
            copy.wait_send()

    for copy in loads[:4]:
        copy.wait()
    ring_ops(PLAN[0][:2])
    first(0, c).start()
    for copy in loads[4:10]:
        copy.wait()
    query_copy().start()
    for copy in loads[10:]:
        copy.wait()
    for h in range(1, HEADS):
        first(h, c).start()
    ring_ops(PLAN[0][2:])
    query_copy().wait_recv()

    def step(h, slot, carry):
        t = h * RING + slot

        @pl.when(slot == 0)
        def _():
            top[...] = jnp.full_like(top, -1e30)
            norm[...] = jnp.zeros_like(norm)
            slope[...] = jnp.zeros_like(slope)
            total[...] = jnp.zeros_like(total)
            first(h, 1 - c).wait_recv()

        for when, ops in enumerate(PLAN):
            if 0 < when < HEADS * RING - 1 and when // RING == h and ops:

                @pl.when(t == when)
                def _():
                    ring_ops(ops)

        for s in range(1, 5):

            @pl.when(slot == 2 * s - 1)
            def _():
                twins_arrived(h, s)

        for r, when in ((6, 0), (5, 1), (7, 2), (4, 3), (2, 4), (1, 5), (3, 6)):

            @pl.when(t == when)
            def _():
                weight(r).start()

        @pl.when(t == 18)
        def _():
            for r in range(1, 2 * WIDE):
                weight_got(r).wait_recv()
                weight_twin(r, c).start()

        attend(h, slot)

        @pl.when(slot == 7)
        def _():
            finish_partner(h)
            finish_own()

        return carry

    last = HEADS * RING - 1
    for h in range(HEADS):
        lax.fori_loop(0, RING if h < HEADS - 1 else RING - 1, functools.partial(step, h), 0)
    ring_ops(PLAN[last])
    twins_arrived(2, 4)
    attend(2, 7, 1, 2)
    finish_partner(2)
    attend(2, 7, 0, 1)
    finish_own()
    for r in range(1, 2 * WIDE):
        weight_twin(r, 1 - c).wait_recv()
    project(0, 0, 2 * WIDE)
    for p in range(2):
        hand_on(1, p)
    query_copy().wait_send()
    for h in range(HEADS):
        drain_ring(h)
    drain_weights()
    for p in range(2):
        combine(2, p)
    project(1, 0, 2 * WIDE)
    for p in range(2):
        for h in range(HEADS):
            drain_part(h, p)
        drain_gather(0, p)
        drain_gather(1, p)
    for p in range(2):
        hand_on(2, p)
    project(2, 0, 5)
    project(2, 5, 2 * WIDE)

    for p in range(2):
        drain_gather(2, p)


def local(queries, keys, values, query_tan, key_tan, value_tan, out_weight, gate, gate_tan):
    fixed = (queries, keys, values, query_tan, key_tan, value_tan, out_weight.reshape(HEADS, DH, -1))
    fixed = [pltpu.with_memory_space_constraint(array, pltpu.HBM) for array in fixed]
    rows = queries.shape[0]
    width = gate.shape[0]
    dma = pltpu.SemaphoreType.DMA
    hbm = pl.BlockSpec(memory_space=pltpu.HBM)
    vmem = pl.BlockSpec(memory_space=pltpu.VMEM)
    projected = pl.pallas_call(
        functools.partial(kernel, rows, width),
        out_shape=jax.ShapeDtypeStruct((2 * rows, width), F32),
        in_specs=[hbm] * 7,
        out_specs=vmem,
        scratch_shapes=[
            pltpu.VMEM((HEADS, 2, rows, 2 * DH), BF16),
            pltpu.VMEM((RING, HEADS, 2, 2, rows, 2 * DH), BF16),
            pltpu.VMEM((HEADS, 2 * WIDE, DH, width), BF16),
            pltpu.VMEM((HEADS, 2, rows, 2 * WIDE * DH), BF16),
            pltpu.VMEM((2 * rows, DH), F32),
            pltpu.VMEM((2 * rows, DH), F32),
            pltpu.VMEM((2 * rows, DH), F32),
            pltpu.VMEM((2, 2 * rows, DH), F32),
            pltpu.VMEM((2, rows, DH), F32),
            pltpu.VMEM((rows, DH), F32),
            pltpu.VMEM((rows, DH), F32),
            pltpu.VMEM((HEADS, 2, rows, DH), BF16),
            pltpu.VMEM((HEADS, 2, rows, DH), BF16),
            pltpu.VMEM((HEADS, 2, 8, DH), F32),
            pltpu.VMEM((HEADS, 2, 8, DH), F32),
            dma((6 * HEADS + 1,)),
            dma((2,)),
            dma((2, HEADS, 7)),
            dma((2, HEADS, 7)),
            dma((2, HEADS, 7)),
            dma((2, HEADS, 7)),
            dma((2, HEADS)),
            dma((2 * WIDE,)),
            dma((2 * WIDE,)),
            dma((2 * WIDE,)),
            dma((2 * WIDE,)),
            dma((2, HEADS, 2, 2)),
            dma((HEADS, 2 * WIDE, 2)),
            dma((HEADS, 2 * WIDE, 2)),
        ],
        compiler_params=pltpu.CompilerParams(
            collective_id=0, has_side_effects=True, vmem_limit_bytes=40 << 20
        ),
    )(*fixed)
    plain, tan = projected[:rows], projected[rows:]
    update = (gate[None, :] * plain).astype(BF16)
    update_tan = (gate_tan[None, :] * plain + gate[None, :] * tan).astype(BF16)
    return update, update_tan


def solution(mesh):
    token = P("ctx", "head")
    in_specs = (token,) * 6 + (P("head", None), P("head"), P("head"))
    return jax.shard_map(
        local, mesh=mesh, in_specs=in_specs, out_specs=(token, token), check_vma=False
    )
```

time: 82.5 us -> 79.3 us (0.961)
  Pallas kernels: 80.8 us -> 77.6 us
    pallas_call x1, Pallas kernels: 80.8 us -> 77.6 us  [local(): pl.pallas_call(functools.partial(kernel, rows, width), out_shape=jax.Shap...]
where the time goes in v4:
time: 79.3 us; the launch traced here: 79.2 us
  Pallas kernels  77.6 us (98%)
  other arithmetic  0.87 us (1%)
    pallas_call x1, Pallas kernels, local(): pl.pallas_call(functools.partial(kernel, rows, width), out_shape=jax.Shap...  77.6 us

profile of v4, /device:TPU:1, one launch (start us, length us, event | category | flops | bytes accessed | tf_op | source)
XLA Modules:
  0.0 79.2 jit_solution(209714327152810049)
XLA Ops:
  0.6 0.0 copy-start
  0.6 0.0 copy-start.1
  0.7 77.6 %shard_map.104 = f32[384,640]{1,0:T(8,128)S(1)} custom-call(bf16[192,384]{1,0:T(8,128)(2,1)} %queries.1, bf16[192,384]{1,0:T(8,128)(2,1)} %keys.1, bf16[192,384]{1,0:T(8,128)(2,1)} %values.1, bf16[192,384]{1,0:T(8,128)(2,1)} %query_tan.1, bf16[192,384]{1,0:T(8,128)(2,1)} %key_tan.1, bf16[192,384]{1,0:T(8,128)(2,1)} %value_tan.1, bf16[3,128,5120]{2,1,0:T(8,128)(2,1)} %bitcast.1), custom_call_target="tpu_custom_call" | custom-call | tf_op jit(solution)/shard_map/pallas_call | solution.py:479
  78.3 0.0 copy-done
  78.3 0.0 copy-done.1
  78.3 0.9 %add_convert_fusion = (bf16[192,640]{1,0:T(8,128)(2,1)}, bf16[192,640]{1,0:T(8,128)(2,1)}) fusion(f32[384,640]{1,0:T(8,128)S(1)} %shard_map.104, f32[640]{0:T(1024)S(1)} %copy-done, f32[640]{0:T(1024)S(1)} %copy-done.1), kind=kLoop, calls=%fused_computation | loop fusion | flops 737280 | bytes 1479680 | tf_op jit(solution)/shard_map/convert_element_type | solution.py:521
Async XLA Ops:
  0.6 77.6 %copy-start = (f32[640]{0:T(1024)S(1)}, f32[640]{0:T(1024)}, u32[]{:S(2)}) copy-start(f32[640]{0:T(1024)} %param.17) | copy-start | bytes 7684
  0.6 77.6 %copy-start.1 = (f32[640]{0:T(1024)S(1)}, f32[640]{0:T(1024)}, u32[]{:S(2)}) copy-start(f32[640]{0:T(1024)} %param.16) | copy-start | bytes 7684

commit v5 on v4

--- a/solution.py
+++ b/solution.py
@@ -22,20 +22,20 @@
 SEND, TAKE = 0, 1
 JOIN, PASS = 2, 3
 PLAN = (
-    ((SEND, 0, 1, 0), (SEND, 0, 1, 1), (SEND, 1, 1, 0), (TAKE, 0, 1, 0), (SEND, 0, 2, 0), (TAKE, 0, 1, 1), (SEND, 0, 2, 1), (SEND, 1, 1, 1)),
-    ((TAKE, 1, 1, 0),),
-    (),
-    ((TAKE, 0, 2, 0), (SEND, 0, 3, 0), (SEND, 1, 2, 0), (TAKE, 0, 2, 1), (SEND, 0, 3, 1), (TAKE, 1, 1, 1)),
-    (),
-    ((TAKE, 0, 3, 0), (SEND, 0, 4, 0), (SEND, 1, 2, 1), (SEND, 2, 1, 0), (TAKE, 1, 2, 0), (SEND, 1, 3, 0), (SEND, 2, 1, 1), (TAKE, 0, 3, 1), (TAKE, 0, 4, 0)),
-    (),
-    ((TAKE, 1, 2, 1), (SEND, 1, 3, 1)),
-    (),
-    (),
-    ((TAKE, 2, 1, 0), (SEND, 2, 2, 0)),
-    (),
-    (),
-    ((TAKE, 1, 3, 0), (SEND, 1, 4, 0), (JOIN, 0), (TAKE, 2, 1, 1), (SEND, 2, 2, 1), (TAKE, 1, 3, 1), (TAKE, 2, 2, 0), (SEND, 2, 3, 0)),
+    ((SEND, 0, 1, 0), (SEND, 1, 1, 0), (SEND, 0, 1, 1), (TAKE, 0, 1, 0), (SEND, 0, 2, 0), (SEND, 1, 1, 1), (TAKE, 1, 1, 0)),
+    ((TAKE, 0, 1, 1), (SEND, 0, 2, 1), (TAKE, 0, 2, 0), (SEND, 0, 3, 0), (SEND, 2, 1, 0)),
+    (),
+    ((TAKE, 1, 1, 1), (TAKE, 0, 2, 1), (SEND, 0, 3, 1), (TAKE, 0, 3, 0), (SEND, 0, 4, 0), (SEND, 1, 2, 0), (SEND, 1, 2, 1), (SEND, 2, 1, 1)),
+    (),
+    ((TAKE, 2, 1, 0), (TAKE, 0, 3, 1), (TAKE, 0, 4, 0)),
+    (),
+    ((TAKE, 1, 2, 0), (SEND, 1, 3, 0)),
+    (),
+    (),
+    ((TAKE, 1, 2, 1), (SEND, 1, 3, 1), (SEND, 2, 2, 0)),
+    ((TAKE, 2, 1, 1),),
+    (),
+    ((JOIN, 0), (TAKE, 1, 3, 0), (SEND, 1, 4, 0), (SEND, 2, 2, 1), (TAKE, 1, 3, 1), (TAKE, 2, 2, 0), (SEND, 2, 3, 0)),
     (),
     ((TAKE, 1, 4, 0), (TAKE, 2, 2, 1), (SEND, 2, 3, 1)),
     ((PASS, 0),),
@@ -376,7 +376,7 @@
 
     for copy in loads[:4]:
         copy.wait()
-    ring_ops(PLAN[0][:2])
+    ring_ops(PLAN[0][:1])
     first(0, c).start()
     for copy in loads[4:10]:
         copy.wait()
@@ -385,7 +385,7 @@
         copy.wait()
     for h in range(1, HEADS):
         first(h, c).start()
-    ring_ops(PLAN[0][2:])
+    ring_ops(PLAN[0][1:])
     query_copy().wait_recv()
 
     def step(h, slot, carry):
@@ -435,7 +435,8 @@
 
     last = HEADS * RING - 1
     for h in range(HEADS):
-        lax.fori_loop(0, RING if h < HEADS - 1 else RING - 1, functools.partial(step, h), 0)
+        for slot in range(RING if h < HEADS - 1 else RING - 1):
+            step(h, slot, 0)
     ring_ops(PLAN[last])
     twins_arrived(2, 4)
     attend(2, 7, 1, 2)

time: 79.3 us -> 77.7 us (0.980)
  Pallas kernels: 77.6 us -> 76.1 us
    pallas_call x1, Pallas kernels: 77.6 us -> 76.1 us  [local(): pl.pallas_call(functools.partial(kernel, rows, width), out_shape=jax.Shap...]
where the time goes in v5:
time: 77.7 us; the launch traced here: 77.6 us
  Pallas kernels  76.1 us (98%)
  other arithmetic  0.87 us (1%)
    pallas_call x1, Pallas kernels, local(): pl.pallas_call(functools.partial(kernel, rows, width), out_shape=jax.Shap...  76.1 us

profile of v5, /device:TPU:1, one launch (start us, length us, event | category | flops | bytes accessed | tf_op | source)
XLA Modules:
  0.0 77.6 jit_solution(14081642420170420468)
XLA Ops:
  0.6 0.0 copy-start
  0.6 0.0 copy-start.1
  0.7 76.1 %shard_map.104 = f32[384,640]{1,0:T(8,128)S(1)} custom-call(bf16[192,384]{1,0:T(8,128)(2,1)} %queries.1, bf16[192,384]{1,0:T(8,128)(2,1)} %keys.1, bf16[192,384]{1,0:T(8,128)(2,1)} %values.1, bf16[192,384]{1,0:T(8,128)(2,1)} %query_tan.1, bf16[192,384]{1,0:T(8,128)(2,1)} %key_tan.1, bf16[192,384]{1,0:T(8,128)(2,1)} %value_tan.1, bf16[3,128,5120]{2,1,0:T(8,128)(2,1)} %bitcast.1), custom_call_target="tpu_custom_call" | custom-call | tf_op jit(solution)/shard_map/pallas_call | solution.py:480
  76.7 0.0 copy-done
  76.8 0.0 copy-done.1
  76.8 0.9 %add_convert_fusion = (bf16[192,640]{1,0:T(8,128)(2,1)}, bf16[192,640]{1,0:T(8,128)(2,1)}) fusion(f32[384,640]{1,0:T(8,128)S(1)} %shard_map.104, f32[640]{0:T(1024)S(1)} %copy-done, f32[640]{0:T(1024)S(1)} %copy-done.1), kind=kLoop, calls=%fused_computation | loop fusion | flops 737280 | bytes 1479680 | tf_op jit(solution)/shard_map/convert_element_type | solution.py:522
Async XLA Ops:
  0.6 76.1 %copy-start = (f32[640]{0:T(1024)S(1)}, f32[640]{0:T(1024)}, u32[]{:S(2)}) copy-start(f32[640]{0:T(1024)} %param.17) | copy-start | bytes 7684
  0.6 76.1 %copy-start.1 = (f32[640]{0:T(1024)S(1)}, f32[640]{0:T(1024)}, u32[]{:S(2)}) copy-start(f32[640]{0:T(1024)} %param.16) | copy-start | bytes 7684

commit v6 on v5

--- a/solution.py
+++ b/solution.py
@@ -336,12 +336,18 @@
         for leg in straight:
             attention_copy(h, leg, p).start()
 
-    def hand_on(h, p):
+    def hand_on_x(h, p):
         attention_got(h, 4, p).wait_recv()
         for leg in onward[:2]:
             attention_copy(h, leg, p).start()
+
+    def hand_on_y(h, p):
         attention_got(h, 2, p).wait_recv()
         attention_copy(h, onward[2], p).start()
+
+    def hand_on(h, p):
+        hand_on_x(h, p)
+        hand_on_y(h, p)
 
     def project(h, low, high):
         for r in range(low, high):
@@ -461,7 +467,9 @@
         drain_gather(0, p)
         drain_gather(1, p)
     for p in range(2):
-        hand_on(2, p)
+        hand_on_x(2, p)
+    for p in range(2):
+        hand_on_y(2, p)
     project(2, 0, 5)
     project(2, 5, 2 * WIDE)
 

time: 77.7 us -> 78.8 us (1.014)
  Pallas kernels: 76.1 us -> 77.1 us
    pallas_call x1, Pallas kernels: 76.1 us -> 77.1 us  [local(): pl.pallas_call(functools.partial(kernel, rows, width), out_shape=jax.Shap...]
where the time goes in v6:
time: 78.8 us; the launch traced here: 78.7 us
  Pallas kernels  77.1 us (98%)
  other arithmetic  0.87 us (1%)
    pallas_call x1, Pallas kernels, local(): pl.pallas_call(functools.partial(kernel, rows, width), out_shape=jax.Shap...  77.1 us

profile of v6, /device:TPU:1, one launch (start us, length us, event | category | flops | bytes accessed | tf_op | source)
XLA Modules:
  0.0 78.7 jit_solution(8670958449491730612)
XLA Ops:
  0.6 0.0 copy-start
  0.6 0.0 copy-start.1
  0.7 77.1 %shard_map.104 = f32[384,640]{1,0:T(8,128)S(1)} custom-call(bf16[192,384]{1,0:T(8,128)(2,1)} %queries.1, bf16[192,384]{1,0:T(8,128)(2,1)} %keys.1, bf16[192,384]{1,0:T(8,128)(2,1)} %values.1, bf16[192,384]{1,0:T(8,128)(2,1)} %query_tan.1, bf16[192,384]{1,0:T(8,128)(2,1)} %key_tan.1, bf16[192,384]{1,0:T(8,128)(2,1)} %value_tan.1, bf16[3,128,5120]{2,1,0:T(8,128)(2,1)} %bitcast.1), custom_call_target="tpu_custom_call" | custom-call | tf_op jit(solution)/shard_map/pallas_call | solution.py:488
  77.8 0.0 copy-done
  77.8 0.0 copy-done.1
  77.8 0.9 %add_convert_fusion = (bf16[192,640]{1,0:T(8,128)(2,1)}, bf16[192,640]{1,0:T(8,128)(2,1)}) fusion(f32[384,640]{1,0:T(8,128)S(1)} %shard_map.104, f32[640]{0:T(1024)S(1)} %copy-done, f32[640]{0:T(1024)S(1)} %copy-done.1), kind=kLoop, calls=%fused_computation | loop fusion | flops 737280 | bytes 1479680 | tf_op jit(solution)/shard_map/convert_element_type | solution.py:530
Async XLA Ops:
  0.6 77.1 %copy-start = (f32[640]{0:T(1024)S(1)}, f32[640]{0:T(1024)}, u32[]{:S(2)}) copy-start(f32[640]{0:T(1024)} %param.17) | copy-start | bytes 7684
  0.6 77.1 %copy-start.1 = (f32[640]{0:T(1024)S(1)}, f32[640]{0:T(1024)}, u32[]{:S(2)}) copy-start(f32[640]{0:T(1024)} %param.16) | copy-start | bytes 7684
